TPU v7x, 32 devices: a whole 2x2x4 slice. The times are simulated.
32 devices in a mesh: row: 4 (over z), col: 8 (over y, x, core).
Axes of the slice: x: 2, y: 2, z: 4, core: 2. Of those that a mesh axis runs over, the one named last changes fastest.
Arguments:
- features: bfloat16 [8192, 512], P(('row', 'col')), may hold values from -6 to 6
- cotangent: bfloat16 [8192, 512], P(('row', 'col')), may hold values from -6 to 6
- weights: bfloat16 [512, 512], replicated, may hold values from -0.25 to 0.25
- bias_term: float32 [512], replicated, may hold values from -3 to 3
- adjacency: bfloat16 [4, 8, 128, 128, 128], P('row', 'col'), may hold values from -0.109375 to 0.109375
- tile_rows: int32 [4, 8, 128], P('row', 'col'), may hold values from 0 to 15, as said below
- tile_cols: int32 [4, 8, 128], P('row', 'col'), may hold values from 0 to 7
- tile_count: int32 [4, 8], P('row', 'col'), may hold values from 25 to 128, as said below
Outputs:
- activated: bfloat16 [8192, 512], P(('row', 'col'))
- grad_input: bfloat16 [8192, 512], P(('row', 'col'))
- grad_weight: float32 [512, 512], replicated
- grad_bias: float32 [512], replicated
Inputs may be any that keep to these rules, and one draw needn't show every extreme that they name: Within one device the pairs (tile_rows, tile_cols) over all 128 slots are distinct. Only the first tile_count slots of a device are in use; some device uses all 128.
All inputs are finite; a program needn't handle non-finite values.
Results may differ from a plain program's by a relative error of at most 0.006.
Values may be sent and summed in bfloat16 or wider, within the bound.
A program may use at most 128 MiB of HBM per device.

v0:
```python
import math

import jax
import jax.numpy as jnp
from jax import lax
from jax.sharding import PartitionSpec as P

TBLK = 16


def aggregate(tile_data, seg_ids, src_ids, in_count, source, seg_count, flipped):
    tile_size = tile_data.shape[-1]
    feat_width = source.shape[1]
    src_blocks = source.reshape(-1, tile_size, feat_width)
    pattern = "tji,tjf->tif" if flipped else "tij,tjf->tif"
    slot_range = jnp.arange(TBLK, dtype=jnp.int32)

    def accumulate(turn_index, running):
        first = turn_index * TBLK
        part_tiles = lax.dynamic_slice_in_dim(tile_data, first, TBLK, 0)
        part_seg = lax.dynamic_slice_in_dim(seg_ids, first, TBLK, 0)
        part_src = lax.dynamic_slice_in_dim(src_ids, first, TBLK, 0)
        picked = src_blocks[part_src]
        products = jnp.einsum(pattern, part_tiles, picked, preferred_element_type=jnp.float32)
        in_use = (first + slot_range < in_count).astype(jnp.float32)
        return running.at[part_seg].add(products * in_use[:, None, None])

    used_blocks = (in_count + TBLK - 1) // TBLK
    running = lax.fori_loop(
        0, used_blocks, accumulate, jnp.zeros((seg_count, tile_size, feat_width), jnp.float32)
    )
    return running.reshape(seg_count * tile_size, feat_width)


def slope_of(shifted, cotangent):
    sig = jax.nn.sigmoid(shifted)
    return (cotangent.astype(jnp.float32) * sig * (1.0 + shifted * (1.0 - sig))).astype(
        jnp.bfloat16
    )


def on_device(features, cotangent, weights, bias_term, adjacency, tile_rows, tile_cols, tile_count):
    tile_size = adjacency.shape[-1]
    slot_total = adjacency.shape[2]
    tile_data = adjacency.reshape(slot_total, tile_size, tile_size)
    row_ids = tile_rows.reshape(slot_total)
    col_ids = tile_cols.reshape(slot_total)
    in_count = tile_count.reshape(())
    n_row = lax.axis_size("row")
    n_col = lax.axis_size("col")
    own_rows = features.shape[0]
    own_blocks = own_rows // tile_size
    node_scale = 1.0 / math.sqrt(own_rows * n_row * n_col)
    projected = jnp.dot(features, weights, preferred_element_type=jnp.float32).astype(jnp.bfloat16)
    gathered = lax.all_gather(projected, "row", axis=0, tiled=True)
    partial_rows = aggregate(
        tile_data, row_ids, col_ids, in_count, gathered, n_col * own_blocks, False
    )
    bias_row = bias_term[None, :]
    shifted = lax.psum_scatter(partial_rows, "col", scatter_dimension=0, tiled=True) + bias_row
    slope_own = slope_of(shifted, cotangent)
    slope_rows = lax.all_gather(slope_own, "col", axis=0, tiled=True)
    activated = jax.nn.silu(shifted).astype(jnp.bfloat16)
    bias_part = jnp.sum(slope_own.astype(jnp.float32), axis=0)
    partial_cols = aggregate(
        tile_data, col_ids, row_ids, in_count, slope_rows, n_row * own_blocks, True
    )
    back = lax.psum_scatter(partial_cols, "row", scatter_dimension=0, tiled=True).astype(
        jnp.bfloat16
    )
    grad_input = lax.dot_general(
        back, weights, (((1,), (1,)), ((), ())), preferred_element_type=jnp.float32
    ).astype(jnp.bfloat16)
    weight_part = lax.dot_general(
        features, back, (((0,), (0,)), ((), ())), preferred_element_type=jnp.float32
    )
    weight_sum, bias_sum = lax.psum((weight_part, bias_part), ("row", "col"))
    return (activated, grad_input, weight_sum * node_scale, bias_sum * node_scale)


def solution(mesh):
    return jax.shard_map(
        on_device,
        mesh=mesh,
        in_specs=(
            P(("row", "col"), None),
            P(("row", "col"), None),
            P(),
            P(),
            P("row", "col", None, None, None),
            P("row", "col", None),
            P("row", "col", None),
            P("row", "col"),
        ),
        out_specs=(P(("row", "col"), None), P(("row", "col"), None), P(), P()),
        check_vma=False,
    )
```

profile of v0, /device:TPU:0, one launch (start us, length us, event | category | flops | bytes accessed | tf_op | source)
XLA Modules:
  0.0 557.2 jit_solution(12842708564158503340)
XLA Ops:
  8.2 2.0 convolution_convert_fusion.1
  10.9 30.1 %all-gather.3.cloned.1.call-done = bf16[1024,512]{1,0:T(8,128)(2,1)} async-done(((bf16[256,512]{1,0:T(8,128)(2,1)}), bf16[1024,512]{1,0:T(8,128)(2,1)}) %all-gather.3.cloned.1.call-update) | async-done | bytes 1048592 | tf_op jit(solution)/shard_map/all_gather | solution.py:55
  41.0 2.5 broadcast_in_dim.21
  43.5 47.8 %while.22 = (s32[]{:T(128)}, f32[16,128,512]{2,1,0:T(8,128)}, s32[]{:T(128)}, s32[128]{0:T(128)S(1)}, bf16[128,128,128]{2,1,0:T(8,128)(2,1)}, /*index=5*/s32[128...) while((s32[]{:T(128)}, f32[16,128,512]{2,1,0:T(8,128)}, ...), condition=%wide.region_2.3_spmd.clone, body=%wide.region_0.2_spmd.clone.sunk | while | flops 270533792 | bytes 23597820 | solution.py:29
  43.6 1.9 gather_fusion
  46.1 3.7 convolution_multiply_fusion.4
  49.8 9.7 %scatter_fusion = f32[16,128,512]{2,1,0:T(8,128)} fusion(f32[16,128,512]{2,1,0:T(8,128)} %get-tuple-element.312, s32[16]{0:T(128)S(1)} %get-tuple-element.287, f32[16,128,512]{2,1,0:T(8,128)} %convolution_multiply_fusion.4), kind=kCustom, calls=%fused_computation.2.clone.clone.1 | custom fusion | flops 1048576 | bytes 12582976 | tf_op jit(solution)/shard_map/while/body/scatter-add | solution.py:26
  59.6 1.9 gather_fusion
  62.1 3.7 convolution_multiply_fusion.4
  65.8 9.6 %scatter_fusion = f32[16,128,512]{2,1,0:T(8,128)} fusion(f32[16,128,512]{2,1,0:T(8,128)} %get-tuple-element.312, s32[16]{0:T(128)S(1)} %get-tuple-element.287, f32[16,128,512]{2,1,0:T(8,128)} %convolution_multiply_fusion.4), kind=kCustom, calls=%fused_computation.2.clone.clone.1 | custom fusion | flops 1048576 | bytes 12582976 | tf_op jit(solution)/shard_map/while/body/scatter-add | solution.py:26
  75.5 1.9 gather_fusion
  78.1 3.7 convolution_multiply_fusion.4
  81.8 9.5 %scatter_fusion = f32[16,128,512]{2,1,0:T(8,128)} fusion(f32[16,128,512]{2,1,0:T(8,128)} %get-tuple-element.312, s32[16]{0:T(128)S(1)} %get-tuple-element.287, f32[16,128,512]{2,1,0:T(8,128)} %convolution_multiply_fusion.4), kind=kCustom, calls=%fused_computation.2.clone.clone.1 | custom fusion | flops 1048576 | bytes 12582976 | tf_op jit(solution)/shard_map/while/body/scatter-add | solution.py:26
  91.3 127.6 %reduce-scatter.3.cloned.1.call-done = f32[256,512]{1,0:T(8,128)} async-done(((f32[2048,512]{1,0:T(8,128)}), f32[256,512]{1,0:T(8,128)}) %reduce-scatter.3.cloned.1.call-update) | async-done | bytes 524304 | tf_op jit(solution)/shard_map/reduce_scatter | solution.py:60
  219.0 2.1 convert_reduce_fusion
  221.1 6.4 %copy.12 = bf16[1,1,128,128,128]{3,4,2,1,0:T(8,128)(2,1)} copy(bf16[1,1,128,128,128]{4,3,2,1,0:T(8,128)(2,1)} %bitcast.27) | data formatting | bytes 8388608 | tf_op args[4]
  227.5 22.0 %all-gather.5.cloned.1.call-done = bf16[2048,512]{1,0:T(8,128)(2,1)} async-done(((bf16[256,512]{1,0:T(8,128)(2,1)}), bf16[2048,512]{1,0:T(8,128)(2,1)}) %all-gather.5.cloned.1.call-update) | async-done | bytes 2097168 | tf_op jit(solution)/shard_map/all_gather | solution.py:62
  249.8 44.9 %while.23 = (s32[]{:T(128)}, f32[8,128,512]{2,1,0:T(8,128)S(1)}, s32[]{:T(128)}, s32[128]{0:T(128)S(1)}, bf16[128,128,128]{1,2,0:T(8,128)(2,1)}, /*index=5*/s32[...) while((s32[]{:T(128)}, f32[8,128,512]{2,1,0:T(8,128)S(1)}, ...), condition=%wide.region_6.7_spmd.clone, body=%wide.region_4.6_spmd.clone.sunk | while | flops 270533792 | bytes 23597820 | solution.py:29
  249.9 3.6 gather_fusion.1
  254.2 4.4 convolution_multiply_fusion.5
  258.6 6.1 %scatter_fusion.1 = f32[8,128,512]{2,1,0:T(8,128)S(1)} fusion(f32[8,128,512]{2,1,0:T(8,128)S(1)} %get-tuple-element.348, s32[16]{0:T(128)S(1)} %get-tuple-element.297, f32[16,128,512]{2,1,0:T(8,128)} %convolution_multiply_fusion.5), kind=kCustom, calls=%fused_computation.3.clone.clone.1 | custom fusion | flops 1048576 | bytes 12582976 | tf_op jit(solution)/shard_map/while/body/scatter-add | solution.py:26
  264.9 3.6 gather_fusion.1
  269.1 4.4 convolution_multiply_fusion.5
  273.6 6.2 %scatter_fusion.1 = f32[8,128,512]{2,1,0:T(8,128)S(1)} fusion(f32[8,128,512]{2,1,0:T(8,128)S(1)} %get-tuple-element.348, s32[16]{0:T(128)S(1)} %get-tuple-element.297, f32[16,128,512]{2,1,0:T(8,128)} %convolution_multiply_fusion.5), kind=kCustom, calls=%fused_computation.3.clone.clone.1 | custom fusion | flops 1048576 | bytes 12582976 | tf_op jit(solution)/shard_map/while/body/scatter-add | solution.py:26
  279.9 3.6 gather_fusion.1
  284.1 4.4 convolution_multiply_fusion.5
  288.6 6.2 %scatter_fusion.1 = f32[8,128,512]{2,1,0:T(8,128)S(1)} fusion(f32[8,128,512]{2,1,0:T(8,128)S(1)} %get-tuple-element.348, s32[16]{0:T(128)S(1)} %get-tuple-element.297, f32[16,128,512]{2,1,0:T(8,128)} %convolution_multiply_fusion.5), kind=kCustom, calls=%fused_computation.3.clone.clone.1 | custom fusion | flops 1048576 | bytes 12582976 | tf_op jit(solution)/shard_map/while/body/scatter-add | solution.py:26
  296.2 116.9 %reduce-scatter.5.cloned.1.call-done = f32[256,512]{1,0:T(8,128)} async-done(((f32[1024,512]{1,0:T(8,128)}), f32[256,512]{1,0:T(8,128)}) %reduce-scatter.5.cloned.1.call-update) | async-done | bytes 524304 | tf_op jit(solution)/shard_map/reduce_scatter | solution.py:68
  413.0 2.3 convolution_bitcast_fusion
  415.4 39.8 %psum.15 = f32[512]{0:T(512)S(1)} all-reduce(f32[512]{0:T(512)S(1)} %get-tuple-element.184), channel_id=1, replica_groups=mesh['row'=4,'col'=8] {'row','col'}, use_global_device_ids=true, to_apply=%region_10.11 | all-reduce | flops 512 | bytes 4096 | tf_op jit(solution)/shard_map/psum | solution.py:77
  455.7 2.1 convolution_convert_fusion
  457.8 90.2 %all-reduce.2.cloned.1.call-done = f32[512,512]{0,1:T(8,128)} async-done(((f32[512,512]{0,1:T(8,128)}), f32[512,512]{0,1:T(8,128)}) %all-reduce.2.cloned.1.call-update) | async-done | bytes 1048592 | tf_op jit(solution)/shard_map/psum | solution.py:77
  (46 shorter events, 10.5 us)
Async XLA Ops:
  7.2 1.0 copy-start
  7.2 36.3 %copy-start.4 = (s32[1,1,128]{2,1,0:T(1,128)S(1)}, s32[1,1,128]{2,1,0:T(1,128)}, u32[]{:S(2)}) copy-start(s32[1,1,128]{2,1,0:T(1,128)} %param.17) | copy-start | bytes 1540
  7.2 36.3 %copy-start.5 = (s32[1,1,128]{2,1,0:T(1,128)S(1)}, s32[1,1,128]{2,1,0:T(1,128)}, u32[]{:S(2)}) copy-start(s32[1,1,128]{2,1,0:T(1,128)} %param.18) | copy-start | bytes 1540
  7.2 33.8 %all-gather.3.cloned.1.call-start = ((), (), s32[]{:S(2)}) async-start(), calls=%async_computation.2 | async-start | bytes 1310720 | tf_op jit(solution)/shard_map/all_gather | solution.py:55
  10.2 208.8 %reduce-scatter.3.cloned.1.call-start = ((), (), s32[]{:S(2)}) async-start(), calls=%async_computation.3 | async-start | bytes 4718592 | tf_op jit(solution)/shard_map/reduce_scatter | solution.py:60
  91.3 127.7 %copy-start.3 = (bf16[256,512]{1,0:T(8,128)(2,1)S(1)}, bf16[256,512]{1,0:T(8,128)(2,1)}, u32[]{:S(2)}) copy-start(bf16[256,512]{1,0:T(8,128)(2,1)} %param.13) | copy-start | bytes 786436
  91.3 127.7 %copy-start.6 = (f32[512]{0:T(512)S(1)}, f32[512]{0:T(512)}, u32[]{:S(2)}) copy-start(f32[512]{0:T(512)} %param.15) | copy-start | bytes 6148
  91.3 158.2 %all-gather.5.cloned.1.call-start = ((), (), s32[]{:S(2)}) async-start(), calls=%async_computation.4 | async-start | bytes 2359296 | tf_op jit(solution)/shard_map/all_gather | solution.py:62
  221.1 191.9 %reduce-scatter.5.cloned.1.call-start = ((), (), s32[]{:S(2)}) async-start(), calls=%async_computation.5 | async-start | bytes 2621440 | tf_op jit(solution)/shard_map/reduce_scatter | solution.py:68
  249.8 163.3 %copy-start.2 = (bf16[256,512]{1,0:T(8,128)(2,1)S(1)}, bf16[256,512]{1,0:T(8,128)(2,1)}, u32[]{:S(2)}) copy-start(bf16[256,512]{1,0:T(8,128)(2,1)} %param.12) | copy-start | bytes 786436
  294.7 1.4 copy-start.1
  296.1 251.9 %all-reduce.2.cloned.1.call-start = ((), (), s32[]{:S(2)}) async-start(), calls=%async_computation.6 | async-start | bytes 2097152 | tf_op jit(solution)/shard_map/psum | solution.py:77
Sparse Core Ops, SparseCore 0:
  10.3 30.6 all-gather.2
  91.4 127.5 reduce-scatter.2
  221.6 27.8 all-gather.4
  296.2 116.7 reduce-scatter.4
  418.6 129.3 all-reduce.1
where the time goes:
time: 559 us; the launch traced here: 557 us
  waiting for transfers between devices  387 us (69%)
  other arithmetic  55.6 us (10%)
  blocking collectives  39.8 us (7%)
  matrix products  30.8 us (6%)
  local copies, waits for them, and re-layouts  29.3 us (5%)
  between operations  14.5 us (3%)
    reduce_scatter x1, waiting for transfers between devices, on_device(): lax.psum_scatter(partial_rows, 'col', scatter_dimension=0, tiled=True)  128 us
    reduce_scatter x1, waiting for transfers between devices, on_device(): lax.psum_scatter(partial_cols, 'row', scatter_dimension=0, tiled=True)  117 us
    psum x1, waiting for transfers between devices, on_device(): weight_sum, bias_sum = lax.psum((weight_part, bias_part), ('row', 'col'))  90.2 us
    scatter-add x6, other arithmetic, accumulate(): return running.at[part_seg].add(products * in_use[:, None, None])  47.2 us
    psum x1, blocking collectives, on_device(): weight_sum, bias_sum = lax.psum((weight_part, bias_part), ('row', 'col'))  39.8 us
    all_gather x1, waiting for transfers between devices, on_device(): gathered = lax.all_gather(projected, 'row', axis=0, tiled=True)  30.1 us
    dot_general x6, matrix products, accumulate(): jnp.einsum(pattern, part_tiles, picked, preferred_element_type=jnp.float32)  24.4 us
    all_gather x1, waiting for transfers between devices, on_device(): slope_rows = lax.all_gather(slope_own, 'col', axis=0, tiled=True)  22 us
  transfers between devices with their start and end apart: 5, of which 5 were waited for; matrix products, arithmetic and copies ran while one was open for 2% of the time, Pallas kernels for 0%

commit v1 on v0

v1 whole, which is shorter than its diff:
```python
import functools
import math

import jax
import jax.numpy as jnp
from jax import lax
from jax.experimental import pallas as pl
from jax.experimental.pallas import tpu as pltpu
from jax.sharding import PartitionSpec as P

MESH = pl.DeviceIdType.MESH
NCH = 4


def kernel(
    R, C, tile, cap, scale,
    feat, cot, w_ref, bias, inv, adj_hbm,
    act, gin, gw, gb,
    adj_v, A, proj, s1, r1, p1, s2, r2, ST, pc, sbR, sbL, rsR, rsL, XT, bp, gacc,
    wsend, wrecv, zsum, fin,
    adj_sem, zrs, zrr, zls, zlr, c1s, c1r, c2s, c2r, ags, agr, ocs, ocr,
    rrs, rrr, rls, rlr, wss, wsr, zss, zsr, fns, fnr,
):
    B, F = feat.shape
    w = F // NCH
    Q = C // 2
    RW = F // C
    K = B // tile
    z = lax.axis_index("row")
    c = lax.axis_index("col")
    core = lax.rem(c, 2)
    q = c // 2
    partner = (z, q * 2 + 1 - core)

    def at_q(d):
        return (z, lax.rem(q + d, Q) * 2 + core)

    def at_c(e):
        return (z, lax.rem(c + e, C))

    def at_z(e):
        return (lax.rem(z + e, R), c)

    adj_copy = pltpu.make_async_copy(adj_hbm, adj_v.at[pl.ds(0, cap)], adj_sem)
    adj_copy.start()

    barrier = pltpu.get_barrier_semaphore()
    for e in range(1, C):
        pl.semaphore_signal(barrier, inc=1, device_id=at_c(e), device_id_type=MESH)
    for e in range(1, R):
        pl.semaphore_signal(barrier, inc=1, device_id=at_z(e), device_id_type=MESH)

    def rcopy(src, dst, ss, rs, dev):
        return pltpu.make_async_remote_copy(
            src_ref=src, dst_ref=dst, send_sem=ss, recv_sem=rs, device_id=dev, device_id_type=MESH
        )

    def z_right(k, m, slot):
        return rcopy(proj.at[k, slot], proj.at[k, slot], zrs.at[k, m], zrr.at[k, m], (lax.rem(z + 1, R), c))

    def z_left(k, m, slot):
        return rcopy(proj.at[k, slot], proj.at[k, slot], zls.at[k, m], zlr.at[k, m], (lax.rem(z + R - 1, R), c))

    def core_sum(k):
        return rcopy(s1.at[k], r1.at[k], c1s.at[k], c1r.at[k], partner)

    def chip_sum(k, d):
        return rcopy(s2.at[k, d], r2.at[k, d], c2s.at[k, d], c2r.at[k, d], at_q(d))

    def slope_chip(k, d, slot):
        return rcopy(ST.at[k, slot], ST.at[k, slot], ags.at[k, d], agr.at[k, d], at_q(d))

    def slope_core(k, d, slot):
        return rcopy(ST.at[k, slot], ST.at[k, slot], ocs.at[k, d], ocr.at[k, d], partner)

    def back_right(k, t):
        return rcopy(sbR.at[k, t], rsR.at[k, t], rrs.at[k, t], rrr.at[k, t], (lax.rem(z + 1, R), c))

    def back_left(k, t):
        return rcopy(sbL.at[k, t], rsL.at[k, t], rls.at[k, t], rlr.at[k, t], (lax.rem(z + R - 1, R), c))

    def weight_part(k, e, src, slot):
        return rcopy(wsend.at[k, src], wrecv.at[k, slot], wss.at[k, e], wsr.at[k, e], at_c(e))

    def weight_z(k, e, slot):
        return rcopy(zsum.at[k, slot], zsum.at[k, slot], zss.at[k, e], zsr.at[k, e], at_z(e))

    def weight_all(k, e, slot):
        return rcopy(fin.at[k, slot], fin.at[k, slot], fns.at[k, e], fnr.at[k, e], at_c(e))

    def cols(k):
        return pl.ds(pl.multiple_of(k * w, w), w)

    full = jnp.dot(feat[...], w_ref[...], preferred_element_type=jnp.float32).astype(jnp.bfloat16)
    for k in range(NCH):
        proj[k, z] = full[:, k * w:(k + 1) * w]
    pl.semaphore_wait(barrier, C + R - 2)

    def send_own(k):
        @pl.when(z + 1 < R)
        def _():
            z_right(k, 0, z).start()

        @pl.when(z >= 1)
        def _():
            z_left(k, 0, z).start()

    send_own(0)
    XT[...] = feat[...].astype(jnp.float32).T.astype(jnp.bfloat16)
    gacc[...] = jnp.zeros_like(gacc)
    adj_v[cap] = jnp.zeros((tile, tile), jnp.bfloat16)
    adj_copy.wait()

    @pl.loop(0, C * K)
    def _(rb):
        for cb in range(R * K):
            A[pl.ds(pl.multiple_of(rb * tile, tile), tile), cb * tile:(cb + 1) * tile] = adj_v[
                inv[rb * (R * K) + cb]
            ]

    def relay(k, m):
        @pl.when(z - 1 - m >= 0)
        def _():
            slot = lax.rem(z - 1 - m + R, R)
            z_right(k, m, slot).wait_recv()
            if m + 1 < R - 1:
                @pl.when(z + 1 < R)
                def _():
                    z_right(k, m + 1, slot).start()

        @pl.when(z + 1 + m < R)
        def _():
            slot = lax.rem(z + 1 + m, R)
            z_left(k, m, slot).wait_recv()
            if m + 1 < R - 1:
                @pl.when(z >= 1)
                def _():
                    z_left(k, m + 1, slot).start()

    def forward(k):
        source = proj[k].reshape(R * B, w)

        def rows_of(c2):
            return A[pl.ds(pl.multiple_of(c2 * B, B), B), :]

        @pl.loop(0, Q)
        def _(j):
            s1[k, j] = jnp.dot(
                rows_of(2 * j + 1 - core), source, preferred_element_type=jnp.float32
            ).astype(jnp.bfloat16)

        core_sum(k).start()

        @pl.loop(0, Q)
        def _(j):
            p1[k, j] = jnp.dot(rows_of(2 * j + core), source, preferred_element_type=jnp.float32)

    def chip_send(k):
        core_sum(k).wait_recv()
        for d in range(1, Q):
            j = lax.rem(q + d, Q)
            s2[k, d] = (p1[k, j] + r1[k, j].astype(jnp.float32)).astype(jnp.bfloat16)
            chip_sum(k, d).start()

    def activate(k):
        total = p1[k, q] + r1[k, q].astype(jnp.float32)
        for d in range(1, Q):
            chip_sum(k, d).wait_recv()
            total = total + r2[k, d].astype(jnp.float32)
        shifted = total + bias[:, cols(k)]
        sig = jax.nn.sigmoid(shifted)
        slope = cot[:, cols(k)].astype(jnp.float32) * sig * (1.0 + shifted * (1.0 - sig))
        slope = slope.astype(jnp.bfloat16).astype(jnp.float32)
        ST[k, c] = slope.T.astype(jnp.bfloat16)
        for d in range(1, Q):
            slope_chip(k, d, c).start()
        slope_core(k, 0, c).start()
        act[:, cols(k)] = (shifted * sig).astype(jnp.bfloat16)
        bp[k] = jnp.sum(slope, axis=0, keepdims=True)

    def backward(k):
        for d in range(1, Q):
            slot = lax.rem(q - d + Q, Q) * 2 + core
            slope_chip(k, d, slot).wait_recv()
            slope_core(k, d, slot).start()
        for d in range(Q):
            slot = lax.rem(q - d + Q, Q) * 2 + 1 - core
            slope_core(k, d, slot).wait_recv()

        @pl.loop(0, R)
        def _(t):
            acc = jnp.zeros((w, B), jnp.float32)
            for j in range(C):
                acc = acc + jnp.dot(
                    ST[k, j],
                    A[j * B:(j + 1) * B, pl.ds(pl.multiple_of(t * B, B), B)],
                    preferred_element_type=jnp.float32,
                )
            pc[k, t] = acc

    def back_sum(k):
        for j in range(R - 1):
            t = R - 1 - j

            @pl.when((z >= 1) & (z <= t))
            def _():
                back_right(k, t).wait_recv()

            @pl.when((z >= 1) & (z < t))
            def _():
                sbR[k, t] = (pc[k, t] + rsR[k, t].astype(jnp.float32)).astype(jnp.bfloat16)

            @pl.when(z == 0)
            def _():
                sbR[k, t] = pc[k, t].astype(jnp.bfloat16)

            @pl.when(z < t)
            def _():
                back_right(k, t).start()

            u = j

            @pl.when((z < R - 1) & (z >= u))
            def _():
                back_left(k, u).wait_recv()

            @pl.when((z < R - 1) & (z > u))
            def _():
                sbL[k, u] = (pc[k, u] + rsL[k, u].astype(jnp.float32)).astype(jnp.bfloat16)

            @pl.when(z == R - 1)
            def _():
                sbL[k, u] = pc[k, u].astype(jnp.bfloat16)

            @pl.when(z > u)
            def _():
                back_left(k, u).start()

    def finish(k):
        @pl.when(z >= 1)
        def _():
            pc[k, z] = pc[k, z] + rsR[k, z].astype(jnp.float32)

        @pl.when(z < R - 1)
        def _():
            pc[k, z] = pc[k, z] + rsL[k, z].astype(jnp.float32)

        back = pc[k, z].T.astype(jnp.bfloat16)
        part = jnp.dot(XT[...], back, preferred_element_type=jnp.float32)
        wsend[k, :, 0:RW, :] = part.astype(jnp.bfloat16).reshape(C, RW, w)
        wsend[k, :, RW:RW + 16, :] = jnp.broadcast_to(bp[k].astype(jnp.bfloat16)[None], (C, 16, w))
        for e in range(1, C):
            weight_part(k, e, lax.rem(c + e, C), c).start()
        wrecv[k, c] = wsend[k, c]
        gacc[...] += lax.dot_general(
            back, w_ref[:, cols(k)], (((1,), (1,)), ((), ())), preferred_element_type=jnp.float32
        )

    def weight_sum(k):
        for e in range(1, C):
            weight_part(k, e, 0, lax.rem(c - e + C, C)).wait_recv()
        total = wrecv[k, 0].astype(jnp.float32)
        for j in range(1, C):
            total = total + wrecv[k, j].astype(jnp.float32)
        zsum[k, z] = total.astype(jnp.bfloat16)
        for e in range(1, R):
            weight_z(k, e, z).start()

    def weight_total(k):
        for e in range(1, R):
            weight_z(k, e, lax.rem(z - e + R, R)).wait_recv()
        total = zsum[k, 0].astype(jnp.float32)
        for j in range(1, R):
            total = total + zsum[k, j].astype(jnp.float32)
        total = total * scale
        fin[k, c] = total[0:RW].astype(jnp.bfloat16)
        for e in range(1, C):
            weight_all(k, e, c).start()
        gb[:, cols(k)] = total[RW:RW + 1]

    def weight_out(k):
        for e in range(1, C):
            weight_all(k, e, lax.rem(c - e + C, C)).wait_recv()
        gw[:, cols(k)] = fin[k].astype(jnp.float32).reshape(F, w)

    first = R - 2
    stages = [forward, chip_send, activate, backward, back_sum, finish, weight_sum, weight_total, weight_out]

    @pl.loop(0, NCH + first + len(stages) - 1)
    def _(i):
        @pl.when(i + 1 < NCH)
        def _():
            send_own(i + 1)

        for m in range(R - 1):
            @pl.when((i - m >= 0) & (i - m < NCH))
            def _():
                relay(i - m, m)

        for order, stage in reversed(list(enumerate(stages))):
            at = i - first - order

            @pl.when((at >= 0) & (at < NCH))
            def _():
                stage(at)

    gin[...] = gacc[...].astype(jnp.bfloat16)

    @pl.loop(0, NCH)
    def _(k):
        for m in range(R - 1):
            @pl.when((z - m >= 0) & (z + 1 < R))
            def _():
                z_right(k, m, z).wait_send()

            @pl.when((z + m < R) & (z >= 1))
            def _():
                z_left(k, m, z).wait_send()
        core_sum(k).wait_send()
        for d in range(1, Q):
            chip_sum(k, d).wait_send()
            slope_chip(k, d, c).wait_send()
        for d in range(Q):
            slope_core(k, d, c).wait_send()
        for j in range(R - 1):
            @pl.when(z < R - 1 - j)
            def _():
                back_right(k, R - 1 - j).wait_send()

            @pl.when(z > j)
            def _():
                back_left(k, j).wait_send()
        for e in range(1, C):
            weight_part(k, e, 0, c).wait_send()
            weight_all(k, e, c).wait_send()
        for e in range(1, R):
            weight_z(k, e, z).wait_send()


def on_device(R, C, features, cotangent, weights, bias_term, adjacency, tile_rows, tile_cols, tile_count):
    tile = adjacency.shape[-1]
    cap = adjacency.shape[2]
    B, F = features.shape
    K = B // tile
    Q = C // 2
    w = F // NCH
    RW = F // C
    pairs = C * K * R * K
    slots = jnp.arange(cap, dtype=jnp.int32)
    pair = tile_rows.reshape(cap) * (R * K) + tile_cols.reshape(cap)
    pair = jnp.where(slots < tile_count.reshape(()), pair, -1)
    hit = jnp.arange(pairs, dtype=jnp.int32)[:, None] == pair[None, :]
    inv = cap + jnp.sum(jnp.where(hit, slots[None, :] - cap, 0), axis=1, dtype=jnp.int32)
    bf, f32 = jnp.bfloat16, jnp.float32
    vmem = pl.BlockSpec(memory_space=pltpu.VMEM)
    V = pltpu.VMEM

    def sems(n):
        return pltpu.SemaphoreType.DMA((NCH, n))

    act, gin, gw, gb = pl.pallas_call(
        functools.partial(kernel, R, C, tile, cap, 1.0 / math.sqrt(B * R * C)),
        out_shape=(
            jax.ShapeDtypeStruct((B, F), bf),
            jax.ShapeDtypeStruct((B, F), bf),
            jax.ShapeDtypeStruct((F, F), f32),
            jax.ShapeDtypeStruct((1, F), f32),
        ),
        in_specs=[vmem] * 4 + [pl.BlockSpec(memory_space=pltpu.SMEM), pl.BlockSpec(memory_space=pl.ANY)],
        out_specs=(vmem,) * 4,
        scratch_shapes=[
            V((cap + 1, tile, tile), bf),
            V((C * B, R * B), bf),
            V((NCH, R, B, w), bf),
            V((NCH, Q, B, w), bf),
            V((NCH, Q, B, w), bf),
            V((NCH, Q, B, w), f32),
            V((NCH, Q, B, w), bf),
            V((NCH, Q, B, w), bf),
            V((NCH, C, w, B), bf),
            V((NCH, R, w, B), f32),
            V((NCH, R, w, B), bf),
            V((NCH, R, w, B), bf),
            V((NCH, R, w, B), bf),
            V((NCH, R, w, B), bf),
            V((F, B), bf),
            V((NCH, 1, w), f32),
            V((B, F), f32),
            V((NCH, C, RW + 16, w), bf),
            V((NCH, C, RW + 16, w), bf),
            V((NCH, R, RW + 16, w), bf),
            V((NCH, C, RW, w), bf),
            pltpu.SemaphoreType.DMA,
            sems(R), sems(R), sems(R), sems(R),
            pltpu.SemaphoreType.DMA((NCH,)), pltpu.SemaphoreType.DMA((NCH,)),
            sems(Q), sems(Q), sems(Q), sems(Q), sems(Q), sems(Q),
            sems(R), sems(R), sems(R), sems(R),
            sems(C), sems(C), sems(R), sems(R), sems(C), sems(C),
        ],
        compiler_params=pltpu.CompilerParams(
            collective_id=0, has_side_effects=True, vmem_limit_bytes=60 * 1024 * 1024
        ),
    )(features, cotangent, weights, bias_term[None, :], inv, adjacency.reshape(cap, tile, tile))
    return act, gin, gw, gb.reshape(F)


def solution(mesh):
    return jax.shard_map(
        functools.partial(on_device, mesh.shape["row"], mesh.shape["col"]),
        mesh=mesh,
        in_specs=(
            P(("row", "col"), None),
            P(("row", "col"), None),
            P(),
            P(),
            P("row", "col", None, None, None),
            P("row", "col", None),
            P("row", "col", None),
            P("row", "col"),
        ),
        out_specs=(P(("row", "col"), None), P(("row", "col"), None), P(), P()),
        check_vma=False,
    )
```

time: 559 us -> 186 us (0.33)
  waiting for transfers between devices: 387 us -> 0 us
  Pallas kernels: 0 us -> 176 us
  other arithmetic: 55.6 us -> 1.31 us
  blocking collectives: 39.8 us -> 0 us
  matrix products: 30.8 us -> 0 us
  local copies, waits for them, and re-layouts: 29.3 us -> 6.84 us
  between operations: 14.5 us -> 1.29 us
    reduce_scatter x2 -> x0, waiting for transfers between devices: 245 us -> none  [the longest x1 128 us: on_device(): lax.psum_scatter(partial_rows, 'col', scatter_dimension=0, tiled=True)]
    pallas_call x0 -> x1, Pallas kernels: none -> 176 us  [on_device(): pl.pallas_call(functools.partial(kernel, R, C, tile, cap, 1.0 / math.sqrt...]
    psum x1 -> x0, waiting for transfers between devices: 90.2 us -> none  [on_device(): weight_sum, bias_sum = lax.psum((weight_part, bias_part), ('row', 'col'))]
    all_gather x2 -> x0, waiting for transfers between devices: 52.1 us -> none  [the longest x1 30.1 us: on_device(): gathered = lax.all_gather(projected, 'row', axis=0, tiled=True)]
    scatter-add x6 -> x0, other arithmetic: 47.2 us -> none  [accumulate(): return running.at[part_seg].add(products * in_use[:, None, None])]
    psum x1 -> x0, blocking collectives: 39.8 us -> none  [on_device(): weight_sum, bias_sum = lax.psum((weight_part, bias_part), ('row', 'col'))]
    dot_general x9 -> x0, matrix products: 30.8 us -> none  [the longest x6 24.4 us: accumulate(): jnp.einsum(pattern, part_tiles, picked, preferred_element_type=jnp.float32)]
    gather x6 -> x0, local copies, waits for them, and re-layouts: 16.5 us -> none  [accumulate(): picked = src_blocks[part_src]]
  transfers between devices with their start and end apart: 5 -> 0, of which waited for: 5 -> 0; matrix products, arithmetic and copies ran while one was open for 2% -> 0% of each run, Pallas kernels for 0% -> 0%
where the time goes in v1:
time: 186 us
  Pallas kernels  176 us (95%)
  local copies, waits for them, and re-layouts  6.84 us (4%)
    pallas_call x1, Pallas kernels, on_device(): pl.pallas_call(functools.partial(kernel, R, C, tile, cap, 1.0 / math.sqrt...  176 us
    unnamed x4, local copies, waits for them, and re-layouts  6.84 us

profile of v1, /device:TPU:0, one launch (start us, length us, event | category | flops | bytes accessed | tf_op | source)
XLA Modules:
  0.0 185.5 jit_solution(6577290495611348788)
XLA Ops:
  1.3 0.7 compare_select_fusion
  2.0 0.1 select_reduce_fusion
  2.1 0.5 broadcast_add_fusion.inv
  2.6 176.1 %shard_map.111 = (bf16[256,512]{1,0:T(8,128)(2,1)}, bf16[256,512]{1,0:T(8,128)(2,1)}, f32[512,512]{1,0:T(8,128)}, f32[1,512]{1,0:T(1,128)}) custom-call(bf16[256,512]{1,0:T(8,128)(2,1)} %feat.1, bf16[256,512]{1,0:T(8,128)(2,1)} %cot.1, bf16[512,512]{1,0:T(8,128)(2,1)} %w_ref.1, f32[1,512]{1,0:T(1,128)} %bitcast.8, s32[128]{0:T(128)} %broadcast_add_fusion.inv, ...), custom_call_target="tpu_custom_call" | custom-call | tf_op jit(solution)/shard_map/pallas_call | solution.py:361
  178.7 1.7 copy.17
  180.3 1.7 copy.18
  182.0 2.3 %copy.19 = f32[512,512]{1,0:T(8,128)} copy(f32[512,512]{1,0:T(8,128)} %get-tuple-element.20) | data formatting | bytes 2097152
  184.3 1.2 copy.20

commit v2 on v1

--- a/solution.py
+++ b/solution.py
@@ -198,43 +198,35 @@
                 )
             pc[k, t] = acc
 
-    def back_sum(k):
-        for j in range(R - 1):
-            t = R - 1 - j
-
-            @pl.when((z >= 1) & (z <= t))
-            def _():
-                back_right(k, t).wait_recv()
-
-            @pl.when((z >= 1) & (z < t))
-            def _():
-                sbR[k, t] = (pc[k, t] + rsR[k, t].astype(jnp.float32)).astype(jnp.bfloat16)
-
-            @pl.when(z == 0)
-            def _():
-                sbR[k, t] = pc[k, t].astype(jnp.bfloat16)
-
-            @pl.when(z < t)
-            def _():
-                back_right(k, t).start()
-
-            u = j
-
-            @pl.when((z < R - 1) & (z >= u))
-            def _():
-                back_left(k, u).wait_recv()
-
-            @pl.when((z < R - 1) & (z > u))
-            def _():
-                sbL[k, u] = (pc[k, u] + rsL[k, u].astype(jnp.float32)).astype(jnp.bfloat16)
-
-            @pl.when(z == R - 1)
-            def _():
-                sbL[k, u] = pc[k, u].astype(jnp.bfloat16)
-
-            @pl.when(z > u)
-            def _():
-                back_left(k, u).start()
+    def back_hop(j):
+        def hop(k):
+            @pl.when(z == j)
+            def _():
+                for t in range(R - 1, j - 1, -1):
+                    if j >= 1:
+                        back_right(k, t).wait_recv()
+                    if t > j:
+                        total = pc[k, t]
+                        if j >= 1:
+                            total = total + rsR[k, t].astype(jnp.float32)
+                        sbR[k, t] = total.astype(jnp.bfloat16)
+                        back_right(k, t).start()
+
+            me = R - 1 - j
+
+            @pl.when(z == me)
+            def _():
+                for t in range(0, me + 1):
+                    if me < R - 1:
+                        back_left(k, t).wait_recv()
+                    if t < me:
+                        total = pc[k, t]
+                        if me < R - 1:
+                            total = total + rsL[k, t].astype(jnp.float32)
+                        sbL[k, t] = total.astype(jnp.bfloat16)
+                        back_left(k, t).start()
+
+        return hop
 
     def finish(k):
         @pl.when(z >= 1)
@@ -284,7 +276,7 @@
         gw[:, cols(k)] = fin[k].astype(jnp.float32).reshape(F, w)
 
     first = R - 2
-    stages = [forward, chip_send, activate, backward, back_sum, finish, weight_sum, weight_total, weight_out]
+    stages = [forward, chip_send, activate, backward] + [back_hop(j) for j in range(R)] + [finish, weight_sum, weight_total, weight_out]
 
     @pl.loop(0, NCH + first + len(stages) - 1)
     def _(i):

time: 186 us -> 99.6 us (0.54)
  Pallas kernels: 176 us -> 89.9 us
    pallas_call x1, Pallas kernels: 176 us -> 89.9 us  [on_device(): pl.pallas_call(functools.partial(kernel, R, C, tile, cap, 1.0 / math.sqrt...]
where the time goes in v2:
time: 99.6 us; the launch traced here: 99.4 us
  Pallas kernels  89.9 us (90%)
  local copies, waits for them, and re-layouts  6.84 us (7%)
  other arithmetic  1.31 us (1%)
  between operations  1.29 us (1%)
    pallas_call x1, Pallas kernels, on_device(): pl.pallas_call(functools.partial(kernel, R, C, tile, cap, 1.0 / math.sqrt...  89.9 us
    unnamed x4, local copies, waits for them, and re-layouts  6.84 us

profile of v2, /device:TPU:0, one launch (start us, length us, event | category | flops | bytes accessed | tf_op | source)
XLA Modules:
  0.0 99.4 jit_solution(9567023534346665899)
XLA Ops:
  1.3 0.7 compare_select_fusion
  2.0 0.1 select_reduce_fusion
  2.1 0.5 broadcast_add_fusion.inv
  2.6 89.9 %shard_map.111 = (bf16[256,512]{1,0:T(8,128)(2,1)}, bf16[256,512]{1,0:T(8,128)(2,1)}, f32[512,512]{1,0:T(8,128)}, f32[1,512]{1,0:T(1,128)}) custom-call(bf16[256,512]{1,0:T(8,128)(2,1)} %feat.1, bf16[256,512]{1,0:T(8,128)(2,1)} %cot.1, bf16[512,512]{1,0:T(8,128)(2,1)} %w_ref.1, f32[1,512]{1,0:T(1,128)} %bitcast.8, s32[128]{0:T(128)} %broadcast_add_fusion.inv, ...), custom_call_target="tpu_custom_call" | custom-call | tf_op jit(solution)/shard_map/pallas_call | solution.py:353
  92.5 1.7 %copy.17 = bf16[256,512]{1,0:T(8,128)(2,1)} copy(bf16[256,512]{1,0:T(8,128)(2,1)} %get-tuple-element.18) | data formatting | bytes 524288
  94.2 1.7 %copy.18 = bf16[256,512]{1,0:T(8,128)(2,1)} copy(bf16[256,512]{1,0:T(8,128)(2,1)} %get-tuple-element.19) | data formatting | bytes 524288
  95.8 2.3 %copy.19 = f32[512,512]{1,0:T(8,128)} copy(f32[512,512]{1,0:T(8,128)} %get-tuple-element.20) | data formatting | bytes 2097152
  98.1 1.2 %copy.20 = f32[512]{0:T(512)} copy(f32[512]{0:T(512)} %bitcast.9) | data formatting | bytes 4096

commit v3 on v2

--- a/solution.py
+++ b/solution.py
@@ -9,7 +9,7 @@
 from jax.sharding import PartitionSpec as P
 
 MESH = pl.DeviceIdType.MESH
-NCH = 4
+NCH = 2
 
 
 def kernel(
@@ -65,13 +65,13 @@
         return rcopy(s1.at[k], r1.at[k], c1s.at[k], c1r.at[k], partner)
 
     def chip_sum(k, d):
-        return rcopy(s2.at[k, d], r2.at[k, d], c2s.at[k, d], c2r.at[k, d], at_q(d))
+        return rcopy(s2.at[k, d], r2.at[k, d], c2s.at[k], c2r.at[k], at_q(d))
 
     def slope_chip(k, d, slot):
         return rcopy(ST.at[k, slot], ST.at[k, slot], ags.at[k, d], agr.at[k, d], at_q(d))
 
-    def slope_core(k, d, slot):
-        return rcopy(ST.at[k, slot], ST.at[k, slot], ocs.at[k, d], ocr.at[k, d], partner)
+    def slope_core(k, slot):
+        return rcopy(ST.at[k, slot], ST.at[k, slot], ocs.at[k], ocr.at[k], partner)
 
     def back_right(k, t):
         return rcopy(sbR.at[k, t], rsR.at[k, t], rrs.at[k, t], rrr.at[k, t], (lax.rem(z + 1, R), c))
@@ -80,13 +80,28 @@
         return rcopy(sbL.at[k, t], rsL.at[k, t], rls.at[k, t], rlr.at[k, t], (lax.rem(z + R - 1, R), c))
 
     def weight_part(k, e, src, slot):
-        return rcopy(wsend.at[k, src], wrecv.at[k, slot], wss.at[k, e], wsr.at[k, e], at_c(e))
+        return rcopy(wsend.at[k, src], wrecv.at[k, slot], wss.at[k], wsr.at[k], at_c(e))
 
     def weight_z(k, e, slot):
-        return rcopy(zsum.at[k, slot], zsum.at[k, slot], zss.at[k, e], zsr.at[k, e], at_z(e))
+        return rcopy(zsum.at[k, slot], zsum.at[k, slot], zss.at[k], zsr.at[k], at_z(e))
 
     def weight_all(k, e, slot):
-        return rcopy(fin.at[k, slot], fin.at[k, slot], fns.at[k, e], fnr.at[k, e], at_c(e))
+        return rcopy(fin.at[k, slot], fin.at[k, slot], fns.at[k], fnr.at[k], at_c(e))
+
+    def chip_sum_all(k):
+        return rcopy(s2.at[k, pl.ds(0, Q - 1)], r2.at[k, pl.ds(0, Q - 1)], c2s.at[k], c2r.at[k], partner)
+
+    def slope_core_all(k):
+        return rcopy(ST.at[k, pl.ds(0, Q)], ST.at[k, pl.ds(0, Q)], ocs.at[k], ocr.at[k], partner)
+
+    def weight_part_group(k):
+        return rcopy(wsend.at[k, pl.ds(0, C - 1)], wrecv.at[k, pl.ds(0, C - 1)], wss.at[k], wsr.at[k], partner)
+
+    def weight_z_group(k):
+        return rcopy(zsum.at[k, pl.ds(0, R - 1)], zsum.at[k, pl.ds(0, R - 1)], zss.at[k], zsr.at[k], partner)
+
+    def weight_all_group(k):
+        return rcopy(fin.at[k, pl.ds(0, C - 1)], fin.at[k, pl.ds(0, C - 1)], fns.at[k], fnr.at[k], partner)
 
     def cols(k):
         return pl.ds(pl.multiple_of(k * w, w), w)
@@ -164,8 +179,8 @@
 
     def activate(k):
         total = p1[k, q] + r1[k, q].astype(jnp.float32)
+        chip_sum_all(k).wait_recv()
         for d in range(1, Q):
-            chip_sum(k, d).wait_recv()
             total = total + r2[k, d].astype(jnp.float32)
         shifted = total + bias[:, cols(k)]
         sig = jax.nn.sigmoid(shifted)
@@ -174,7 +189,7 @@
         ST[k, c] = slope.T.astype(jnp.bfloat16)
         for d in range(1, Q):
             slope_chip(k, d, c).start()
-        slope_core(k, 0, c).start()
+        slope_core(k, c).start()
         act[:, cols(k)] = (shifted * sig).astype(jnp.bfloat16)
         bp[k] = jnp.sum(slope, axis=0, keepdims=True)
 
@@ -182,10 +197,8 @@
         for d in range(1, Q):
             slot = lax.rem(q - d + Q, Q) * 2 + core
             slope_chip(k, d, slot).wait_recv()
-            slope_core(k, d, slot).start()
-        for d in range(Q):
-            slot = lax.rem(q - d + Q, Q) * 2 + 1 - core
-            slope_core(k, d, slot).wait_recv()
+            slope_core(k, slot).start()
+        slope_core_all(k).wait_recv()
 
         @pl.loop(0, R)
         def _(t):
@@ -248,9 +261,12 @@
             back, w_ref[:, cols(k)], (((1,), (1,)), ((), ())), preferred_element_type=jnp.float32
         )
 
+        @pl.when(k == NCH - 1)
+        def _():
+            gin[...] = gacc[...].astype(jnp.bfloat16)
+
     def weight_sum(k):
-        for e in range(1, C):
-            weight_part(k, e, 0, lax.rem(c - e + C, C)).wait_recv()
+        weight_part_group(k).wait_recv()
         total = wrecv[k, 0].astype(jnp.float32)
         for j in range(1, C):
             total = total + wrecv[k, j].astype(jnp.float32)
@@ -259,8 +275,7 @@
             weight_z(k, e, z).start()
 
     def weight_total(k):
-        for e in range(1, R):
-            weight_z(k, e, lax.rem(z - e + R, R)).wait_recv()
+        weight_z_group(k).wait_recv()
         total = zsum[k, 0].astype(jnp.float32)
         for j in range(1, R):
             total = total + zsum[k, j].astype(jnp.float32)
@@ -271,9 +286,8 @@
         gb[:, cols(k)] = total[RW:RW + 1]
 
     def weight_out(k):
-        for e in range(1, C):
-            weight_all(k, e, lax.rem(c - e + C, C)).wait_recv()
-        gw[:, cols(k)] = fin[k].astype(jnp.float32).reshape(F, w)
+        weight_all_group(k).wait_recv()
+        gw[:, cols(k)] = fin[k].reshape(F, w)
 
     first = R - 2
     stages = [forward, chip_send, activate, backward] + [back_hop(j) for j in range(R)] + [finish, weight_sum, weight_total, weight_out]
@@ -295,8 +309,6 @@
             @pl.when((at >= 0) & (at < NCH))
             def _():
                 stage(at)
-
-    gin[...] = gacc[...].astype(jnp.bfloat16)
 
     @pl.loop(0, NCH)
     def _(k):
@@ -309,11 +321,10 @@
             def _():
                 z_left(k, m, z).wait_send()
         core_sum(k).wait_send()
+        chip_sum_all(k).wait_send()
         for d in range(1, Q):
-            chip_sum(k, d).wait_send()
             slope_chip(k, d, c).wait_send()
-        for d in range(Q):
-            slope_core(k, d, c).wait_send()
+        slope_core_all(k).wait_send()
         for j in range(R - 1):
             @pl.when(z < R - 1 - j)
             def _():
@@ -322,11 +333,9 @@
             @pl.when(z > j)
             def _():
                 back_left(k, j).wait_send()
-        for e in range(1, C):
-            weight_part(k, e, 0, c).wait_send()
-            weight_all(k, e, c).wait_send()
-        for e in range(1, R):
-            weight_z(k, e, z).wait_send()
+        weight_part_group(k).wait_send()
+        weight_z_group(k).wait_send()
+        weight_all_group(k).wait_send()
 
 
 def on_device(R, C, features, cotangent, weights, bias_term, adjacency, tile_rows, tile_cols, tile_count):
@@ -347,6 +356,8 @@
     vmem = pl.BlockSpec(memory_space=pltpu.VMEM)
     V = pltpu.VMEM
 
+    group = pltpu.SemaphoreType.DMA((NCH,))
+
     def sems(n):
         return pltpu.SemaphoreType.DMA((NCH, n))
 
@@ -355,7 +366,7 @@
         out_shape=(
             jax.ShapeDtypeStruct((B, F), bf),
             jax.ShapeDtypeStruct((B, F), bf),
-            jax.ShapeDtypeStruct((F, F), f32),
+            jax.ShapeDtypeStruct((F, F), bf),
             jax.ShapeDtypeStruct((1, F), f32),
         ),
         in_specs=[vmem] * 4 + [pl.BlockSpec(memory_space=pltpu.SMEM), pl.BlockSpec(memory_space=pl.ANY)],
@@ -384,16 +395,16 @@
             V((NCH, C, RW, w), bf),
             pltpu.SemaphoreType.DMA,
             sems(R), sems(R), sems(R), sems(R),
-            pltpu.SemaphoreType.DMA((NCH,)), pltpu.SemaphoreType.DMA((NCH,)),
-            sems(Q), sems(Q), sems(Q), sems(Q), sems(Q), sems(Q),
+            group, group,
+            group, group, sems(Q), sems(Q), group, group,
             sems(R), sems(R), sems(R), sems(R),
-            sems(C), sems(C), sems(R), sems(R), sems(C), sems(C),
+            group, group, group, group, group, group,
         ],
         compiler_params=pltpu.CompilerParams(
             collective_id=0, has_side_effects=True, vmem_limit_bytes=60 * 1024 * 1024
         ),
     )(features, cotangent, weights, bias_term[None, :], inv, adjacency.reshape(cap, tile, tile))
-    return act, gin, gw, gb.reshape(F)
+    return act, gin, gw.astype(f32), gb.reshape(F)
 
 
 def solution(mesh):

time: 99.6 us -> 103 us (1.034)
  Pallas kernels: 89.9 us -> 93.3 us
  local copies, waits for them, and re-layouts: 6.84 us -> 4.59 us
  other arithmetic: 1.31 us -> 3.45 us
    pallas_call x1, Pallas kernels: 89.9 us -> 93.3 us  [on_device(): pl.pallas_call(functools.partial(kernel, R, C, tile, cap, 1.0 / math.sqrt...]
    unnamed x4 -> x3, local copies, waits for them, and re-layouts: 6.84 us -> 4.59 us
    convert_element_type x0 -> x1, other arithmetic: none -> 2.15 us  [on_device(): return (act, gin, gw.astype(f32), gb.reshape(F))]
where the time goes in v3:
time: 103 us
  Pallas kernels  93.3 us (91%)
  local copies, waits for them, and re-layouts  4.59 us (4%)
  other arithmetic  3.45 us (3%)
  between operations  1.29 us (1%)
    pallas_call x1, Pallas kernels, on_device(): pl.pallas_call(functools.partial(kernel, R, C, tile, cap, 1.0 / math.sqrt...  93.3 us
    unnamed x3, local copies, waits for them, and re-layouts  4.59 us
    convert_element_type x1, other arithmetic, on_device(): return (act, gin, gw.astype(f32), gb.reshape(F))  2.15 us

profile of v3, /device:TPU:0, one launch (start us, length us, event | category | flops | bytes accessed | tf_op | source)
XLA Modules:
  0.0 102.7 jit_solution(7355294041052438184)
XLA Ops:
  1.3 0.7 compare_select_fusion
  2.0 0.1 select_reduce_fusion
  2.1 0.5 broadcast_add_fusion.inv
  2.6 93.3 %shard_map.111 = (bf16[256,512]{1,0:T(8,128)(2,1)}, bf16[256,512]{1,0:T(8,128)(2,1)}, bf16[512,512]{1,0:T(8,128)(2,1)}, f32[1,512]{1,0:T(1,128)}) custom-call(bf16[256,512]{1,0:T(8,128)(2,1)} %feat.1, bf16[256,512]{1,0:T(8,128)(2,1)} %cot.1, bf16[512,512]{1,0:T(8,128)(2,1)} %w_ref.1, f32[1,512]{1,0:T(1,128)} %bitcast.8, s32[128]{0:T(128)} %broadcast_add_fusion.inv, ...), custom_call_target="tpu_custom_call" | custom-call | tf_op jit(solution)/shard_map/pallas_call | solution.py:364
  95.9 2.1 %convert_element_type.3 = f32[512,512]{1,0:T(8,128)} convert(bf16[512,512]{1,0:T(8,128)(2,1)} %get-tuple-element.10) | non-fusion elementwise | flops 262144 | bytes 1572864 | tf_op jit(solution)/shard_map/convert_element_type | solution.py:407
  98.1 1.7 %copy.16 = bf16[256,512]{1,0:T(8,128)(2,1)} copy(bf16[256,512]{1,0:T(8,128)(2,1)} %get-tuple-element.18) | data formatting | bytes 524288
  99.7 1.7 %copy.17 = bf16[256,512]{1,0:T(8,128)(2,1)} copy(bf16[256,512]{1,0:T(8,128)(2,1)} %get-tuple-element.19) | data formatting | bytes 524288
  101.4 1.3 %copy.18 = f32[512]{0:T(512)} copy(f32[512]{0:T(512)} %bitcast.9) | data formatting | bytes 4096

commit v4 on v3

--- a/solution.py
+++ b/solution.py
@@ -9,7 +9,7 @@
 from jax.sharding import PartitionSpec as P
 
 MESH = pl.DeviceIdType.MESH
-NCH = 2
+NCH = 4
 
 
 def kernel(
@@ -193,11 +193,13 @@
         act[:, cols(k)] = (shifted * sig).astype(jnp.bfloat16)
         bp[k] = jnp.sum(slope, axis=0, keepdims=True)
 
-    def backward(k):
+    def slope_pass(k):
         for d in range(1, Q):
             slot = lax.rem(q - d + Q, Q) * 2 + core
             slope_chip(k, d, slot).wait_recv()
             slope_core(k, slot).start()
+
+    def backward(k):
         slope_core_all(k).wait_recv()
 
         @pl.loop(0, R)
@@ -290,9 +292,21 @@
         gw[:, cols(k)] = fin[k].reshape(F, w)
 
     first = R - 2
-    stages = [forward, chip_send, activate, backward] + [back_hop(j) for j in range(R)] + [finish, weight_sum, weight_total, weight_out]
-
-    @pl.loop(0, NCH + first + len(stages) - 1)
+    stages = [(3 + j, back_hop(j)) for j in range(R - 1, 0, -1)]
+    stages += [
+        (2 + R, finish),
+        (3, slope_pass),
+        (2, activate),
+        (1, chip_send),
+        (0, forward),
+        (3, backward),
+        (3, back_hop(0)),
+        (5 + R, weight_out),
+        (4 + R, weight_total),
+        (3 + R, weight_sum),
+    ]
+
+    @pl.loop(0, NCH + first + 5 + R)
     def _(i):
         @pl.when(i + 1 < NCH)
         def _():
@@ -303,8 +317,8 @@
             def _():
                 relay(i - m, m)
 
-        for order, stage in reversed(list(enumerate(stages))):
-            at = i - first - order
+        for after, stage in stages:
+            at = i - first - after
 
             @pl.when((at >= 0) & (at < NCH))
             def _():

time: 103 us -> 94.8 us (0.920)
  Pallas kernels: 93.3 us -> 85.2 us
    pallas_call x1, Pallas kernels: 93.3 us -> 85.2 us  [on_device(): pl.pallas_call(functools.partial(kernel, R, C, tile, cap, 1.0 / math.sqrt...]
where the time goes in v4:
time: 94.8 us; the launch traced here: 94.5 us
  Pallas kernels  85.2 us (90%)
  local copies, waits for them, and re-layouts  4.59 us (5%)
  other arithmetic  3.45 us (4%)
  between operations  1.29 us (1%)
    pallas_call x1, Pallas kernels, on_device(): pl.pallas_call(functools.partial(kernel, R, C, tile, cap, 1.0 / math.sqrt...  85.2 us
    unnamed x3, local copies, waits for them, and re-layouts  4.59 us
    convert_element_type x1, other arithmetic, on_device(): return (act, gin, gw.astype(f32), gb.reshape(F))  2.15 us

profile of v4, /device:TPU:0, one launch (start us, length us, event | category | flops | bytes accessed | tf_op | source)
XLA Modules:
  0.0 94.5 jit_solution(10424684825941219602)
XLA Ops:
  1.3 0.7 compare_select_fusion
  2.0 0.1 select_reduce_fusion
  2.1 0.5 broadcast_add_fusion.inv
  2.6 85.2 %shard_map.111 = (bf16[256,512]{1,0:T(8,128)(2,1)}, bf16[256,512]{1,0:T(8,128)(2,1)}, bf16[512,512]{1,0:T(8,128)(2,1)}, f32[1,512]{1,0:T(1,128)}) custom-call(bf16[256,512]{1,0:T(8,128)(2,1)} %feat.1, bf16[256,512]{1,0:T(8,128)(2,1)} %cot.1, bf16[512,512]{1,0:T(8,128)(2,1)} %w_ref.1, f32[1,512]{1,0:T(1,128)} %bitcast.8, s32[128]{0:T(128)} %broadcast_add_fusion.inv, ...), custom_call_target="tpu_custom_call" | custom-call | tf_op jit(solution)/shard_map/pallas_call | solution.py:378
  87.8 2.1 %convert_element_type.3 = f32[512,512]{1,0:T(8,128)} convert(bf16[512,512]{1,0:T(8,128)(2,1)} %get-tuple-element.10) | non-fusion elementwise | flops 262144 | bytes 1572864 | tf_op jit(solution)/shard_map/convert_element_type | solution.py:421
  89.9 1.7 %copy.16 = bf16[256,512]{1,0:T(8,128)(2,1)} copy(bf16[256,512]{1,0:T(8,128)(2,1)} %get-tuple-element.18) | data formatting | bytes 524288
  91.6 1.7 %copy.17 = bf16[256,512]{1,0:T(8,128)(2,1)} copy(bf16[256,512]{1,0:T(8,128)(2,1)} %get-tuple-element.19) | data formatting | bytes 524288
  93.3 1.3 %copy.18 = f32[512]{0:T(512)} copy(f32[512]{0:T(512)} %bitcast.9) | data formatting | bytes 4096

commit v5 on v4

--- a/solution.py
+++ b/solution.py
@@ -16,10 +16,10 @@
     R, C, tile, cap, scale,
     feat, cot, w_ref, bias, inv, adj_hbm,
     act, gin, gw, gb,
-    adj_v, A, proj, s1, r1, p1, s2, r2, ST, pc, sbR, sbL, rsR, rsL, XT, bp, gacc,
+    adj_v, A, proj, s1, r1, p1, s2, r2, ST, pc, sb, rs, XT, bp, gacc,
     wsend, wrecv, zsum, fin,
-    adj_sem, zrs, zrr, zls, zlr, c1s, c1r, c2s, c2r, ags, agr, ocs, ocr,
-    rrs, rrr, rls, rlr, wss, wsr, zss, zsr, fns, fnr,
+    adj_sem, pjs, pjr, c1s, c1r, c2s, c2r, ags, agr, ocs, ocr,
+    bks, bkr, wss, wsr, zss, zsr, fns, fnr,
 ):
     B, F = feat.shape
     w = F // NCH
@@ -55,11 +55,8 @@
             src_ref=src, dst_ref=dst, send_sem=ss, recv_sem=rs, device_id=dev, device_id_type=MESH
         )
 
-    def z_right(k, m, slot):
-        return rcopy(proj.at[k, slot], proj.at[k, slot], zrs.at[k, m], zrr.at[k, m], (lax.rem(z + 1, R), c))
-
-    def z_left(k, m, slot):
-        return rcopy(proj.at[k, slot], proj.at[k, slot], zls.at[k, m], zlr.at[k, m], (lax.rem(z + R - 1, R), c))
+    def proj_row(k, e):
+        return rcopy(proj.at[k, z], proj.at[k, z], pjs.at[k], pjr.at[k], at_z(e))
 
     def core_sum(k):
         return rcopy(s1.at[k], r1.at[k], c1s.at[k], c1r.at[k], partner)
@@ -73,11 +70,8 @@
     def slope_core(k, slot):
         return rcopy(ST.at[k, slot], ST.at[k, slot], ocs.at[k], ocr.at[k], partner)
 
-    def back_right(k, t):
-        return rcopy(sbR.at[k, t], rsR.at[k, t], rrs.at[k, t], rrr.at[k, t], (lax.rem(z + 1, R), c))
-
-    def back_left(k, t):
-        return rcopy(sbL.at[k, t], rsL.at[k, t], rls.at[k, t], rlr.at[k, t], (lax.rem(z + R - 1, R), c))
+    def back_row(k, e):
+        return rcopy(sb.at[k, e], rs.at[k, e], bks.at[k], bkr.at[k], at_z(e))
 
     def weight_part(k, e, src, slot):
         return rcopy(wsend.at[k, src], wrecv.at[k, slot], wss.at[k], wsr.at[k], at_c(e))
@@ -87,6 +81,12 @@
 
     def weight_all(k, e, slot):
         return rcopy(fin.at[k, slot], fin.at[k, slot], fns.at[k], fnr.at[k], at_c(e))
+
+    def proj_row_all(k):
+        return rcopy(proj.at[k, pl.ds(0, R - 1)], proj.at[k, pl.ds(0, R - 1)], pjs.at[k], pjr.at[k], partner)
+
+    def back_row_all(k):
+        return rcopy(sb.at[k, pl.ds(0, R - 1)], rs.at[k, pl.ds(0, R - 1)], bks.at[k], bkr.at[k], partner)
 
     def chip_sum_all(k):
         return rcopy(s2.at[k, pl.ds(0, Q - 1)], r2.at[k, pl.ds(0, Q - 1)], c2s.at[k], c2r.at[k], partner)
@@ -112,13 +112,8 @@
     pl.semaphore_wait(barrier, C + R - 2)
 
     def send_own(k):
-        @pl.when(z + 1 < R)
-        def _():
-            z_right(k, 0, z).start()
-
-        @pl.when(z >= 1)
-        def _():
-            z_left(k, 0, z).start()
+        for e in range(1, R):
+            proj_row(k, e).start()
 
     send_own(0)
     XT[...] = feat[...].astype(jnp.float32).T.astype(jnp.bfloat16)
@@ -133,26 +128,8 @@
                 inv[rb * (R * K) + cb]
             ]
 
-    def relay(k, m):
-        @pl.when(z - 1 - m >= 0)
-        def _():
-            slot = lax.rem(z - 1 - m + R, R)
-            z_right(k, m, slot).wait_recv()
-            if m + 1 < R - 1:
-                @pl.when(z + 1 < R)
-                def _():
-                    z_right(k, m + 1, slot).start()
-
-        @pl.when(z + 1 + m < R)
-        def _():
-            slot = lax.rem(z + 1 + m, R)
-            z_left(k, m, slot).wait_recv()
-            if m + 1 < R - 1:
-                @pl.when(z >= 1)
-                def _():
-                    z_left(k, m + 1, slot).start()
-
     def forward(k):
+        proj_row_all(k).wait_recv()
         source = proj[k].reshape(R * B, w)
 
         def rows_of(c2):
@@ -202,8 +179,7 @@
     def backward(k):
         slope_core_all(k).wait_recv()
 
-        @pl.loop(0, R)
-        def _(t):
+        def piece(t):
             acc = jnp.zeros((w, B), jnp.float32)
             for j in range(C):
                 acc = acc + jnp.dot(
@@ -211,48 +187,21 @@
                     A[j * B:(j + 1) * B, pl.ds(pl.multiple_of(t * B, B), B)],
                     preferred_element_type=jnp.float32,
                 )
-            pc[k, t] = acc
-
-    def back_hop(j):
-        def hop(k):
-            @pl.when(z == j)
-            def _():
-                for t in range(R - 1, j - 1, -1):
-                    if j >= 1:
-                        back_right(k, t).wait_recv()
-                    if t > j:
-                        total = pc[k, t]
-                        if j >= 1:
-                            total = total + rsR[k, t].astype(jnp.float32)
-                        sbR[k, t] = total.astype(jnp.bfloat16)
-                        back_right(k, t).start()
-
-            me = R - 1 - j
-
-            @pl.when(z == me)
-            def _():
-                for t in range(0, me + 1):
-                    if me < R - 1:
-                        back_left(k, t).wait_recv()
-                    if t < me:
-                        total = pc[k, t]
-                        if me < R - 1:
-                            total = total + rsL[k, t].astype(jnp.float32)
-                        sbL[k, t] = total.astype(jnp.bfloat16)
-                        back_left(k, t).start()
-
-        return hop
+            return acc
+
+        @pl.loop(1, R)
+        def _(e):
+            sb[k, e] = piece(lax.rem(z + e, R)).astype(jnp.bfloat16)
+            back_row(k, e).start()
+
+        pc[k] = piece(z)
 
     def finish(k):
-        @pl.when(z >= 1)
-        def _():
-            pc[k, z] = pc[k, z] + rsR[k, z].astype(jnp.float32)
-
-        @pl.when(z < R - 1)
-        def _():
-            pc[k, z] = pc[k, z] + rsL[k, z].astype(jnp.float32)
-
-        back = pc[k, z].T.astype(jnp.bfloat16)
+        back_row_all(k).wait_recv()
+        total = pc[k]
+        for e in range(1, R):
+            total = total + rs[k, e].astype(jnp.float32)
+        back = total.T.astype(jnp.bfloat16)
         part = jnp.dot(XT[...], back, preferred_element_type=jnp.float32)
         wsend[k, :, 0:RW, :] = part.astype(jnp.bfloat16).reshape(C, RW, w)
         wsend[k, :, RW:RW + 16, :] = jnp.broadcast_to(bp[k].astype(jnp.bfloat16)[None], (C, 16, w))
@@ -291,34 +240,26 @@
         weight_all_group(k).wait_recv()
         gw[:, cols(k)] = fin[k].reshape(F, w)
 
-    first = R - 2
-    stages = [(3 + j, back_hop(j)) for j in range(R - 1, 0, -1)]
-    stages += [
-        (2 + R, finish),
+    stages = [
+        (4, finish),
         (3, slope_pass),
         (2, activate),
         (1, chip_send),
+        (3, backward),
         (0, forward),
-        (3, backward),
-        (3, back_hop(0)),
-        (5 + R, weight_out),
-        (4 + R, weight_total),
-        (3 + R, weight_sum),
+        (7, weight_out),
+        (6, weight_total),
+        (5, weight_sum),
     ]
 
-    @pl.loop(0, NCH + first + 5 + R)
+    @pl.loop(0, NCH + 7)
     def _(i):
         @pl.when(i + 1 < NCH)
         def _():
             send_own(i + 1)
 
-        for m in range(R - 1):
-            @pl.when((i - m >= 0) & (i - m < NCH))
-            def _():
-                relay(i - m, m)
-
         for after, stage in stages:
-            at = i - first - after
+            at = i - after
 
             @pl.when((at >= 0) & (at < NCH))
             def _():
@@ -326,27 +267,13 @@
 
     @pl.loop(0, NCH)
     def _(k):
-        for m in range(R - 1):
-            @pl.when((z - m >= 0) & (z + 1 < R))
-            def _():
-                z_right(k, m, z).wait_send()
-
-            @pl.when((z + m < R) & (z >= 1))
-            def _():
-                z_left(k, m, z).wait_send()
+        proj_row_all(k).wait_send()
         core_sum(k).wait_send()
         chip_sum_all(k).wait_send()
         for d in range(1, Q):
             slope_chip(k, d, c).wait_send()
         slope_core_all(k).wait_send()
-        for j in range(R - 1):
-            @pl.when(z < R - 1 - j)
-            def _():
-                back_right(k, R - 1 - j).wait_send()
-
-            @pl.when(z > j)
-            def _():
-                back_left(k, j).wait_send()
+        back_row_all(k).wait_send()
         weight_part_group(k).wait_send()
         weight_z_group(k).wait_send()
         weight_all_group(k).wait_send()
@@ -395,9 +322,7 @@
             V((NCH, Q, B, w), bf),
             V((NCH, Q, B, w), bf),
             V((NCH, C, w, B), bf),
-            V((NCH, R, w, B), f32),
-            V((NCH, R, w, B), bf),
-            V((NCH, R, w, B), bf),
+            V((NCH, w, B), f32),
             V((NCH, R, w, B), bf),
             V((NCH, R, w, B), bf),
             V((F, B), bf),
@@ -408,10 +333,10 @@
             V((NCH, R, RW + 16, w), bf),
             V((NCH, C, RW, w), bf),
             pltpu.SemaphoreType.DMA,
-            sems(R), sems(R), sems(R), sems(R),
+            group, group,
             group, group,
             group, group, sems(Q), sems(Q), group, group,
-            sems(R), sems(R), sems(R), sems(R),
+            group, group,
             group, group, group, group, group, group,
         ],
         compiler_params=pltpu.CompilerParams(

time: 94.8 us -> 94.1 us (level)
  no operation moved by 1% of the time
where the time goes in v5:
time: 94.1 us; the launch traced here: 93.8 us
  Pallas kernels  84.5 us (90%)
  local copies, waits for them, and re-layouts  4.59 us (5%)
  other arithmetic  3.45 us (4%)
  between operations  1.29 us (1%)
    pallas_call x1, Pallas kernels, on_device(): pl.pallas_call(functools.partial(kernel, R, C, tile, cap, 1.0 / math.sqrt...  84.5 us
    unnamed x3, local copies, waits for them, and re-layouts  4.59 us
    convert_element_type x1, other arithmetic, on_device(): return (act, gin, gw.astype(f32), gb.reshape(F))  2.15 us

profile of v5, /device:TPU:0, one launch (start us, length us, event | category | flops | bytes accessed | tf_op | source)
XLA Modules:
  0.0 93.8 jit_solution(13353477819303662297)
XLA Ops:
  1.3 0.7 compare_select_fusion
  2.0 0.1 select_reduce_fusion
  2.1 0.5 broadcast_add_fusion.inv
  2.6 84.5 %shard_map.111 = (bf16[256,512]{1,0:T(8,128)(2,1)}, bf16[256,512]{1,0:T(8,128)(2,1)}, bf16[512,512]{1,0:T(8,128)(2,1)}, f32[1,512]{1,0:T(1,128)}) custom-call(bf16[256,512]{1,0:T(8,128)(2,1)} %feat.1, bf16[256,512]{1,0:T(8,128)(2,1)} %cot.1, bf16[512,512]{1,0:T(8,128)(2,1)} %w_ref.1, f32[1,512]{1,0:T(1,128)} %bitcast.8, s32[128]{0:T(128)} %broadcast_add_fusion.inv, ...), custom_call_target="tpu_custom_call" | custom-call | tf_op jit(solution)/shard_map/pallas_call | solution.py:305
  87.1 2.1 %convert_element_type.3 = f32[512,512]{1,0:T(8,128)} convert(bf16[512,512]{1,0:T(8,128)(2,1)} %get-tuple-element.10) | non-fusion elementwise | flops 262144 | bytes 1572864 | tf_op jit(solution)/shard_map/convert_element_type | solution.py:346
  89.2 1.7 %copy.16 = bf16[256,512]{1,0:T(8,128)(2,1)} copy(bf16[256,512]{1,0:T(8,128)(2,1)} %get-tuple-element.18) | data formatting | bytes 524288
  90.9 1.7 %copy.17 = bf16[256,512]{1,0:T(8,128)(2,1)} copy(bf16[256,512]{1,0:T(8,128)(2,1)} %get-tuple-element.19) | data formatting | bytes 524288
  92.5 1.3 %copy.18 = f32[512]{0:T(512)} copy(f32[512]{0:T(512)} %bitcast.9) | data formatting | bytes 4096

commit v6 on v5

--- a/solution.py
+++ b/solution.py
@@ -180,14 +180,11 @@
         slope_core_all(k).wait_recv()
 
         def piece(t):
-            acc = jnp.zeros((w, B), jnp.float32)
-            for j in range(C):
-                acc = acc + jnp.dot(
-                    ST[k, j],
-                    A[j * B:(j + 1) * B, pl.ds(pl.multiple_of(t * B, B), B)],
-                    preferred_element_type=jnp.float32,
-                )
-            return acc
+            return jnp.dot(
+                jnp.concatenate([ST[k, j] for j in range(C)], axis=1),
+                A[:, pl.ds(pl.multiple_of(t * B, B), B)],
+                preferred_element_type=jnp.float32,
+            )
 
         @pl.loop(1, R)
         def _(e):
@@ -241,12 +238,12 @@
         gw[:, cols(k)] = fin[k].reshape(F, w)
 
     stages = [
-        (4, finish),
         (3, slope_pass),
         (2, activate),
         (1, chip_send),
         (3, backward),
         (0, forward),
+        (4, finish),
         (7, weight_out),
         (6, weight_total),
         (5, weight_sum),

time: 94.1 us -> 85.1 us (0.904)
  Pallas kernels: 84.5 us -> 75.5 us
    pallas_call x1, Pallas kernels: 84.5 us -> 75.5 us  [on_device(): pl.pallas_call(functools.partial(kernel, R, C, tile, cap, 1.0 / math.sqrt...]
where the time goes in v6:
time: 85.1 us; the launch traced here: 84.9 us
  Pallas kernels  75.5 us (89%)
  local copies, waits for them, and re-layouts  4.59 us (5%)
  other arithmetic  3.45 us (4%)
  between operations  1.29 us (2%)
    pallas_call x1, Pallas kernels, on_device(): pl.pallas_call(functools.partial(kernel, R, C, tile, cap, 1.0 / math.sqrt...  75.5 us
    unnamed x3, local copies, waits for them, and re-layouts  4.59 us
    convert_element_type x1, other arithmetic, on_device(): return (act, gin, gw.astype(f32), gb.reshape(F))  2.15 us

profile of v6, /device:TPU:0, one launch (start us, length us, event | category | flops | bytes accessed | tf_op | source)
XLA Modules:
  0.0 84.9 jit_solution(10745600917372027669)
XLA Ops:
  1.3 0.7 compare_select_fusion
  2.0 0.1 select_reduce_fusion
  2.1 0.5 broadcast_add_fusion.inv
  2.6 75.5 %shard_map.111 = (bf16[256,512]{1,0:T(8,128)(2,1)}, bf16[256,512]{1,0:T(8,128)(2,1)}, bf16[512,512]{1,0:T(8,128)(2,1)}, f32[1,512]{1,0:T(1,128)}) custom-call(bf16[256,512]{1,0:T(8,128)(2,1)} %feat.1, bf16[256,512]{1,0:T(8,128)(2,1)} %cot.1, bf16[512,512]{1,0:T(8,128)(2,1)} %w_ref.1, f32[1,512]{1,0:T(1,128)} %bitcast.8, s32[128]{0:T(128)} %broadcast_add_fusion.inv, ...), custom_call_target="tpu_custom_call" | custom-call | tf_op jit(solution)/shard_map/pallas_call | solution.py:302
  78.1 2.1 %convert_element_type.3 = f32[512,512]{1,0:T(8,128)} convert(bf16[512,512]{1,0:T(8,128)(2,1)} %get-tuple-element.10) | non-fusion elementwise | flops 262144 | bytes 1572864 | tf_op jit(solution)/shard_map/convert_element_type | solution.py:343
  80.3 1.7 %copy.16 = bf16[256,512]{1,0:T(8,128)(2,1)} copy(bf16[256,512]{1,0:T(8,128)(2,1)} %get-tuple-element.18) | data formatting | bytes 524288
  81.9 1.7 %copy.17 = bf16[256,512]{1,0:T(8,128)(2,1)} copy(bf16[256,512]{1,0:T(8,128)(2,1)} %get-tuple-element.19) | data formatting | bytes 524288
  83.6 1.3 %copy.18 = f32[512]{0:T(512)} copy(f32[512]{0:T(512)} %bitcast.9) | data formatting | bytes 4096

commit v7 on v6

--- a/solution.py
+++ b/solution.py
@@ -118,6 +118,7 @@
     send_own(0)
     XT[...] = feat[...].astype(jnp.float32).T.astype(jnp.bfloat16)
     gacc[...] = jnp.zeros_like(gacc)
+    send_own(1)
     adj_v[cap] = jnp.zeros((tile, tile), jnp.bfloat16)
     adj_copy.wait()
 
@@ -251,9 +252,9 @@
 
     @pl.loop(0, NCH + 7)
     def _(i):
-        @pl.when(i + 1 < NCH)
+        @pl.when(i + 2 < NCH)
         def _():
-            send_own(i + 1)
+            send_own(i + 2)
 
         for after, stage in stages:
             at = i - after

time: 85.1 us -> 86.4 us (1.015)
  Pallas kernels: 75.5 us -> 76.7 us
    pallas_call x1, Pallas kernels: 75.5 us -> 76.7 us  [on_device(): pl.pallas_call(functools.partial(kernel, R, C, tile, cap, 1.0 / math.sqrt...]
where the time goes in v7:
time: 86.4 us; the launch traced here: 86.1 us
  Pallas kernels  76.7 us (89%)
  local copies, waits for them, and re-layouts  4.59 us (5%)
  other arithmetic  3.45 us (4%)
  between operations  1.29 us (1%)
    pallas_call x1, Pallas kernels, on_device(): pl.pallas_call(functools.partial(kernel, R, C, tile, cap, 1.0 / math.sqrt...  76.7 us
    unnamed x3, local copies, waits for them, and re-layouts  4.59 us
    convert_element_type x1, other arithmetic, on_device(): return (act, gin, gw.astype(f32), gb.reshape(F))  2.15 us

profile of v7, /device:TPU:0, one launch (start us, length us, event | category | flops | bytes accessed | tf_op | source)
XLA Modules:
  0.0 86.1 jit_solution(7971700569108684399)
XLA Ops:
  1.3 0.7 compare_select_fusion
  2.0 0.1 select_reduce_fusion
  2.1 0.5 broadcast_add_fusion.inv
  2.6 76.7 %shard_map.111 = (bf16[256,512]{1,0:T(8,128)(2,1)}, bf16[256,512]{1,0:T(8,128)(2,1)}, bf16[512,512]{1,0:T(8,128)(2,1)}, f32[1,512]{1,0:T(1,128)}) custom-call(bf16[256,512]{1,0:T(8,128)(2,1)} %feat.1, bf16[256,512]{1,0:T(8,128)(2,1)} %cot.1, bf16[512,512]{1,0:T(8,128)(2,1)} %w_ref.1, f32[1,512]{1,0:T(1,128)} %bitcast.8, s32[128]{0:T(128)} %broadcast_add_fusion.inv, ...), custom_call_target="tpu_custom_call" | custom-call | tf_op jit(solution)/shard_map/pallas_call | solution.py:303
  79.3 2.1 %convert_element_type.3 = f32[512,512]{1,0:T(8,128)} convert(bf16[512,512]{1,0:T(8,128)(2,1)} %get-tuple-element.10) | non-fusion elementwise | flops 262144 | bytes 1572864 | tf_op jit(solution)/shard_map/convert_element_type | solution.py:344
  81.5 1.7 %copy.16 = bf16[256,512]{1,0:T(8,128)(2,1)} copy(bf16[256,512]{1,0:T(8,128)(2,1)} %get-tuple-element.18) | data formatting | bytes 524288
  83.1 1.7 %copy.17 = bf16[256,512]{1,0:T(8,128)(2,1)} copy(bf16[256,512]{1,0:T(8,128)(2,1)} %get-tuple-element.19) | data formatting | bytes 524288
  84.8 1.3 %copy.18 = f32[512]{0:T(512)} copy(f32[512]{0:T(512)} %bitcast.9) | data formatting | bytes 4096
